TPU v7x, 32 devices: a whole 2x2x4 slice. The times are simulated.
32 devices in a mesh: grp: 2 (over x), dev: 4 (over y, core), role: 4 (over z).
Axes of the slice: x: 2, y: 2, z: 4, core: 2. Of those that a mesh axis runs over, the one named last changes fastest.
Arguments:
- queries: bfloat16 [256, 4096], P(('grp', 'dev', 'role')), parts along dimension 0, may hold values from -16 to 16
- key_cache: bfloat16 [256, 128, 512], P(('grp', 'dev', 'role')), parts along dimension 0, may hold values from -8 to 8
- value_cache: bfloat16 [256, 128, 512], P(('grp', 'dev', 'role')), parts along dimension 0, may hold values from -6 to 6
- new_key: bfloat16 [256, 512], P(('grp', 'dev', 'role')), parts along dimension 0, may hold values from -8 to 8
- new_value: bfloat16 [256, 512], P(('grp', 'dev', 'role')), parts along dimension 0, may hold values from -6 to 6
- lengths: int32 [256], P(('grp', 'dev', 'role')), parts along dimension 0, may hold values from 1 to 128, as said below
- residual: bfloat16 [256, 4096], P(('grp', 'dev', 'role')), parts along dimension 0, may hold values from -40 to 40
- out_proj: bfloat16 [4096, 4096], P(None, ('dev', 'role')), may hold values from -0.09375 to 0.09375
- norm_gain: float32 [4096], replicated, may hold values from 0.25 to 1.75
- expert_ids: int32 [256, 8], P(('grp', 'dev', 'role')), parts along dimension 0, may hold values from 0 to 63, all different within a row; in each aligned block of 8 rows (0 to 7, 8 to 15, ...) at most 2 rows name the same one
- gate_weights: float32 [256, 8], P(('grp', 'dev', 'role')), parts along dimension 0, may hold values from 0.03 to 0.6
- w_gate: bfloat16 [128, 4096, 384], P(('dev', 'role')), may hold values from -0.09375 to 0.09375
- w_up: bfloat16 [128, 4096, 384], P(('dev', 'role')), may hold values from -0.09375 to 0.09375
- w_down: bfloat16 [128, 384, 4096], P(('dev', 'role')), may hold values from -0.21875 to 0.21875
Outputs:
- mixed: bfloat16 [256, 4096], P(('grp', 'dev', 'role')), parts along dimension 0
There are 2 independent parts, one for each index of `grp`. A program takes and returns all parts, laid end to end along the dimension named above; an argument that names none is the same for every part. Nothing has to cross between parts.
Inputs may be any that keep to these rules, and one draw needn't show every extreme that they name: `expert_ids`: each row names 8 different experts; among the rows of one device no expert is named more than 2 times, a bound that some block reaches. `lengths`: the first row of each part holds 128 positions.
All inputs are finite; a program needn't handle non-finite values.
Results may differ from a plain program's by a relative error of at most 0.0053.
Values may be sent and summed in bfloat16 or wider, within the bound.
A program may use at most 192 MiB of HBM per device.

v0:
```python
import jax
import jax.numpy as jnp
from jax import lax
from jax.sharding import PartitionSpec as P

QH = 32
KV = 4
HD = 128
EXPERTS = 64
TOP = 8
CTX = 128


def attend_rows(queries, key_cache, value_cache, new_key, new_value, lengths):
    count = queries.shape[0]
    grouped = queries.reshape(count, KV, QH // KV, HD)
    cached_keys = key_cache.reshape(count, CTX, KV, HD)
    cached_values = value_cache.reshape(count, CTX, KV, HD)
    fresh_key = new_key.reshape(count, KV, HD)
    fresh_value = new_value.reshape(count, KV, HD).astype(jnp.float32)
    scaling = HD ** (-0.5)
    scores = (
        jnp.einsum("rkgd,rtkd->rkgt", grouped, cached_keys, preferred_element_type=jnp.float32)
        * scaling
    )
    own_score = (
        jnp.einsum("rkgd,rkd->rkg", grouped, fresh_key, preferred_element_type=jnp.float32)
        * scaling
    )
    visible = jnp.arange(CTX, dtype=jnp.int32)[None, :] < lengths[:, None]
    scores = jnp.where(visible[:, None, None, :], scores, -jnp.inf)
    highest = jnp.maximum(jnp.max(scores, axis=-1), own_score)
    weights = jnp.exp(scores - highest[..., None])
    own_weight = jnp.exp(own_score - highest)
    total = jnp.sum(weights, axis=-1) + own_weight
    probs = (weights / total[..., None]).astype(jnp.bfloat16)
    own_prob = (own_weight / total).astype(jnp.bfloat16)
    combined = jnp.einsum(
        "rkgt,rtkd->rkgd", probs, cached_values, preferred_element_type=jnp.float32
    )
    combined = combined + own_prob.astype(jnp.float32)[..., None] * fresh_value[:, :, None, :]
    return combined.reshape(count, QH * HD).astype(jnp.bfloat16)


def expert_work(inputs, w_gate, w_up, w_down):
    gate_value = jnp.einsum("pscd,sdh->psch", inputs, w_gate, preferred_element_type=jnp.float32)
    up_value = jnp.einsum("pscd,sdh->psch", inputs, w_up, preferred_element_type=jnp.float32)
    activation = (jax.nn.silu(gate_value) * up_value).astype(jnp.bfloat16)
    return jnp.einsum("psch,shd->pscd", activation, w_down, preferred_element_type=jnp.float32)


def body(
    queries,
    key_cache,
    value_cache,
    new_key,
    new_value,
    lengths,
    residual,
    out_proj,
    norm_gain,
    expert_ids,
    gate_weights,
    w_gate,
    w_up,
    w_down,
):
    count = queries.shape[0]
    capacity = count // 4
    width = residual.shape[1]
    attended = attend_rows(queries, key_cache, value_cache, new_key, new_value, lengths)
    columns = jnp.dot(
        lax.all_gather(attended, ("dev", "role"), axis=0, tiled=True),
        out_proj,
        preferred_element_type=jnp.float32,
    )
    projected = lax.all_to_all(columns, ("dev", "role"), split_axis=0, concat_axis=1, tiled=True)
    widened = residual.astype(jnp.float32) + projected
    widened = widened.astype(jnp.bfloat16).astype(jnp.float32)
    normed = (
        widened * lax.rsqrt(jnp.mean(widened * widened, axis=-1, keepdims=True) + 1e-06) * norm_gain
    ).astype(jnp.bfloat16)
    flat_ids = expert_ids.reshape(count * TOP)
    expert_hits = (flat_ids[:, None] == jnp.arange(EXPERTS, dtype=jnp.int32)[None, :]).astype(
        jnp.int32
    )
    slot_index = jnp.sum((jnp.cumsum(expert_hits, axis=0) - 1) * expert_hits, axis=-1)
    position = flat_ids * capacity + slot_index
    placement = (
        position[:, None] == jnp.arange(EXPERTS * capacity, dtype=jnp.int32)[None, :]
    ).astype(jnp.float32)
    placement = placement.reshape(count, TOP, EXPERTS * capacity)
    assign = jnp.sum(placement, axis=1).astype(jnp.bfloat16)
    send_buffer = jnp.einsum(
        "rs,rd->sd", assign, normed, preferred_element_type=jnp.float32
    ).astype(jnp.bfloat16)
    combine_weights = jnp.einsum("rk,rks->rs", gate_weights, placement)
    slots_here = w_gate.shape[0]
    devices = lax.axis_size(("dev", "role"))
    doubled = jnp.broadcast_to(
        send_buffer.reshape(EXPERTS, 1, capacity, width), (EXPERTS, 2, capacity, width)
    )
    outgoing = doubled.reshape(devices, slots_here, capacity, width)
    produced = expert_work(
        lax.all_to_all(outgoing, ("dev", "role"), split_axis=0, concat_axis=0, tiled=True),
        w_gate,
        w_up,
        w_down,
    )
    returned = lax.all_to_all(
        produced.astype(jnp.bfloat16), ("dev", "role"), split_axis=0, concat_axis=0, tiled=True
    ).astype(produced.dtype)
    expert_out = jnp.sum(returned.reshape(EXPERTS, 2, capacity, width), axis=1)
    routed = jnp.dot(
        combine_weights,
        expert_out.reshape(EXPERTS * capacity, width),
        precision=lax.Precision.HIGHEST,
    )
    return (widened + routed).astype(jnp.bfloat16)


def solution(mesh):
    placed = (
        P(("grp", "dev", "role"), None),
        P(("grp", "dev", "role"), None, None),
        P(("grp", "dev", "role"), None, None),
        P(("grp", "dev", "role"), None),
        P(("grp", "dev", "role"), None),
        P(("grp", "dev", "role")),
        P(("grp", "dev", "role"), None),
        P(None, ("dev", "role")),
        P(),
        P(("grp", "dev", "role"), None),
        P(("grp", "dev", "role"), None),
        P(("dev", "role"), None, None),
        P(("dev", "role"), None, None),
        P(("dev", "role"), None, None),
    )
    return jax.shard_map(
        body, mesh=mesh, in_specs=placed, out_specs=P(("grp", "dev", "role"), None), check_vma=False
    )
```

profile of v0, /device:TPU:0, one launch (start us, length us, event | category | flops | bytes accessed | tf_op | source)
XLA Modules:
  0.0 232.2 jit_solution(13601883459734438995)
XLA Ops:
  6.5 0.9 iota_compare_fusion.3
  7.4 0.7 bitcast_convert_fusion
  8.1 1.0 fusion.56
  9.1 2.0 fusion.67
  11.2 0.2 fusion.50
  11.4 1.7 fusion.37
  13.1 0.7 copy.82
  14.3 40.3 %all-gather.2.cloned.1.call-done = bf16[128,4096]{1,0:T(8,128)(2,1)} async-done(((bf16[8,4096]{1,0:T(8,128)(2,1)}), bf16[128,4096]{1,0:T(8,128)(2,1)}) %all-gather.2.cloned.1.call-update) | async-done | bytes 1048592 | tf_op jit(solution)/shard_map/all_gather | solution.py:73
  54.6 2.3 convolution_bitcast_fusion
  56.9 3.6 %all-to-all-start = ((f32[16,8,256]{2,1,0:T(8,128)}), f32[16,8,256]{2,1,0:T(8,128)S(1)}, u32[]{:S(2)}, u32[]{:S(2)}) async-start(f32[16,8,256]{2,1,0:T(8,128)} %convolution_bitcast_fusion), calls=%async_computation | async-start | bytes 262144 | tf_op jit(solution)/shard_map/all_to_all | solution.py:77
  60.6 7.2 %all-to-all-done = f32[16,8,256]{2,1,0:T(8,128)S(1)} async-done(((f32[16,8,256]{2,1,0:T(8,128)}), f32[16,8,256]{2,1,0:T(8,128)S(1)}, u32[]{:S(2)}, u32[]{:S(2)}) %all-to-all-start) | async-done | bytes 131104 | tf_op jit(solution)/shard_map/all_to_all | solution.py:77
  68.1 0.5 convolution_convert_fusion
  68.6 0.7 broadcast_in_dim.18
  69.3 2.5 %broadcast_in_dim.19 = bf16[64,2,2,4096]{3,2,1,0:T(2,128)(2,1)S(1)} broadcast(bf16[64,2,4096]{2,1,0:T(2,128)(2,1)S(1)} %broadcast_in_dim.18), dimensions={0,2,3} | broadcast | bytes 3145728 | tf_op jit(solution)/shard_map/broadcast_in_dim | solution.py:100
  71.8 52.5 %all_to_all.29 = bf16[16,8,2,4096]{3,2,1,0:T(2,128)(2,1)S(1)} all-to-all(bf16[16,8,2,4096]{3,2,1,0:T(2,128)(2,1)S(1)} %bitcast.92), channel_id=1, replica_groups=mesh['grp'=2,'dev'=4,'role'=4] {'dev','role'}, dimensions={0} | all-to-all | bytes 4194304 | tf_op jit(solution)/shard_map/all_to_all | solution.py:105
  124.2 10.4 %fusion.15 = f32[16,8,2,384]{3,0,2,1:T(8,128)S(1)} fusion(bf16[8,4096,384]{2,1,0:T(8,128)(2,1)} %param.25, bf16[16,8,2,4096]{3,2,1,0:T(2,128)(2,1)S(1)} %all_to_all.29), kind=kOutput, calls=%fused_computation.14 | convolution fusion | flops 805306368 | bytes 27656192 | tf_op jit(solution)/shard_map/pscd,sdh->psch/dot_general | solution.py:46
  134.6 21.2 %fusion.9 = bf16[16,8,2,4096]{3,0,2,1:T(8,128)(2,1)} fusion(bf16[8,384,4096]{2,1,0:T(8,128)(2,1)} %param.27, bf16[8,4096,384]{2,1,0:T(8,128)(2,1)} %param.26, bf16[16,8,2,4096]{3,2,1,0:T(2,128)(2,1)S(1)} %all_to_all.29, f32[16,8,2,384]{3,0,2,1:T(8,128)S(1)} %fusion.15), kind=kOutput, calls=%fused_computation.7 | convolution fusion | flops 1612251136 | bytes 54919168 | tf_op jit(solution)/shard_map/psch,shd->pscd/dot_general | solution.py:49
  155.8 5.1 %copy.38 = bf16[16,8,2,4096]{3,2,1,0:T(2,128)(2,1)} copy(bf16[16,8,2,4096]{3,0,2,1:T(8,128)(2,1)} %fusion.9) | data formatting | bytes 4194304 | tf_op jit(solution)/shard_map/convert_element_type | solution.py:111
  160.8 4.1 %all-to-all-start.2 = ((bf16[16,8,2,4096]{3,2,1,0:T(2,128)(2,1)}), bf16[16,8,2,4096]{3,2,1,0:T(2,128)(2,1)S(1)}, u32[]{:S(2)}, u32[]{:S(2)}) async-start(bf16[16,8,2,4096]{3,2,1,0:T(2,128)(2,1)} %copy.38), calls=%async_computation.2 | async-start | bytes 4194304 | tf_op jit(solution)/shard_map/all_to_all | solution.py:110
  164.9 0.2 fusion.59
  165.1 49.0 %all-to-all-done.2 = bf16[16,8,2,4096]{3,2,1,0:T(2,128)(2,1)S(1)} async-done(((bf16[16,8,2,4096]{3,2,1,0:T(2,128)(2,1)}), bf16[16,8,2,4096]{3,2,1,0:T(2,128)(2,1)S(1)}, u32[]{:S(2)}, u32[]{:S(2)}) %all-to-all-start.2) | async-done | bytes 2097184 | tf_op jit(solution)/shard_map/all_to_all | solution.py:110
  214.1 4.1 %convert_reduce_fusion = f32[64,2,4096]{2,1,0:T(2,128)} fusion(bf16[64,2,2,4096]{3,2,1,0:T(2,128)(2,1)S(1)} %bitcast.91), kind=kLoop, calls=%fused_computation.11 | loop fusion | flops 1572864 | bytes 4194304 | tf_op jit(solution)/shard_map/reduce_sum | solution.py:113
  218.2 3.8 %reshape.102 = f32[128,4096]{1,0:T(8,128)} reshape(f32[64,2,4096]{2,1,0:T(2,128)} %convert_reduce_fusion) | data formatting | bytes 4194304 | tf_op jit(solution)/shard_map/reshape | solution.py:116
  222.0 3.3 %fusion.12 = bf16[8,4096]{1,0:T(8,128)(2,1)} fusion(f32[8,128]{1,0:T(8,128)S(1)} %bitcast.99, f32[128,4096]{1,0:T(8,128)} %reshape.102, bf16[8,4096]{1,0:T(8,128)(2,1)S(1)} %get-tuple-element.6), kind=kOutput, calls=%fused_computation.10 | convolution fusion | flops 50429952 | bytes 2232320 | tf_op jit(solution)/shard_map/dot_general | solution.py:114
  (26 shorter events, 0.9 us)
Async XLA Ops:
  6.5 48.1 %copy-start = (bf16[4096,256]{1,0:T(8,128)(2,1)S(1)}, bf16[4096,256]{1,0:T(8,128)(2,1)}, u32[]{:S(2)}) copy-start(bf16[4096,256]{1,0:T(8,128)(2,1)} %param.21) | copy-start | bytes 6291460
  6.5 7.2 %copy-start.4 = (s32[8,8]{1,0:T(8,128)S(1)}, s32[8,8]{1,0:T(8,128)}, u32[]{:S(2)}) copy-start(s32[8,8]{1,0:T(8,128)} %param.23) | copy-start | bytes 772
  6.5 48.0 %all-gather.2.cloned.1.call-start = ((), (), s32[]{:S(2)}) async-start(), calls=%async_computation.3 | async-start | bytes 1114112 | tf_op jit(solution)/shard_map/all_gather | solution.py:73
  13.1 54.8 %copy-start.2 = (bf16[8,4096]{1,0:T(8,128)(2,1)S(1)}, bf16[8,4096]{1,0:T(8,128)(2,1)}, u32[]{:S(2)}) copy-start(bf16[8,4096]{1,0:T(8,128)(2,1)} %param.20) | copy-start | bytes 196612
  13.1 55.0 %copy-start.3 = (f32[4096]{0:T(1024)S(1)}, f32[4096]{0:T(1024)}, u32[]{:S(2)}) copy-start(f32[4096]{0:T(1024)} %param.22) | copy-start | bytes 49156
  56.9 11.0 %all-to-all-start = ((f32[16,8,256]{2,1,0:T(8,128)}), f32[16,8,256]{2,1,0:T(8,128)S(1)}, u32[]{:S(2)}, u32[]{:S(2)}) async-start(f32[16,8,256]{2,1,0:T(8,128)} %convolution_bitcast_fusion), calls=%async_computation | async-start | bytes 262144 | tf_op jit(solution)/shard_map/all_to_all | solution.py:77
  160.8 4.1 %copy-start.5 = (f32[8,8]{1,0:T(8,128)S(1)}, f32[8,8]{1,0:T(8,128)}, u32[]{:S(2)}) copy-start(f32[8,8]{1,0:T(8,128)} %param.24) | copy-start | bytes 772
  160.8 53.2 %all-to-all-start.2 = ((bf16[16,8,2,4096]{3,2,1,0:T(2,128)(2,1)}), bf16[16,8,2,4096]{3,2,1,0:T(2,128)(2,1)S(1)}, u32[]{:S(2)}, u32[]{:S(2)}) async-start(bf16[16,8,2,4096]{3,2,1,0:T(2,128)(2,1)} %copy.38), calls=%async_computation.2 | async-start | bytes 4194304 | tf_op jit(solution)/shard_map/all_to_all | solution.py:110
  218.2 7.1 %copy-start.1 = (bf16[4096,256]{1,0:T(8,128)(2,1)S(1)}, bf16[4096,256]{1,0:T(8,128)(2,1)}, u32[]{:S(2)}) copy-start(bf16[4096,256]{1,0:T(8,128)(2,1)} %param.21) | copy-start | bytes 6291460
Sparse Core Ops, SparseCore 0:
  13.9 40.6 all-gather.1
where the time goes:
time: 233 us; the launch traced here: 232 us
  waiting for transfers between devices  96.5 us (41%)
  blocking collectives  52.5 us (23%)
  matrix products  42.5 us (18%)
  between operations  13.5 us (6%)
  local copies, waits for them, and re-layouts  12.9 us (6%)
  starting transfers between devices  7.69 us (3%)
  other arithmetic  6.58 us (3%)
    all_to_all x1, blocking collectives, body(): lax.all_to_all(outgoing, ('dev', 'role'), split_axis=0, concat_axis=0, ti...  52.5 us
    all_to_all x1, waiting for transfers between devices, body(): lax.all_to_all(produced.astype(jnp.bfloat16), ('dev', 'role'), split_axis...  49 us
    all_gather x1, waiting for transfers between devices, body(): lax.all_gather(attended, ('dev', 'role'), axis=0, tiled=True)  40.3 us
    dot_general x1, matrix products, expert_work(): jnp.einsum('psch,shd->pscd', activation, w_down, preferred_element_type=j...  21.2 us
    dot_general x1, matrix products, expert_work(): jnp.einsum('pscd,sdh->psch', inputs, w_gate, preferred_element_type=jnp.f...  10.4 us
    all_to_all x1, waiting for transfers between devices, body(): lax.all_to_all(columns, ('dev', 'role'), split_axis=0, concat_axis=1, til...  7.25 us
    convert_element_type x1, local copies, waits for them, and re-layouts, body(): produced.astype(jnp.bfloat16)  5.07 us
  transfers between devices with their start and end apart: 3, of which 3 were waited for; matrix products, arithmetic and copies ran while one was open for 0% of the time, Pallas kernels for 0%

commit v1 on v0

--- a/solution.py
+++ b/solution.py
@@ -1,6 +1,10 @@
+import functools
+
 import jax
 import jax.numpy as jnp
 from jax import lax
+from jax.experimental import pallas as pl
+from jax.experimental.pallas import tpu as pltpu
 from jax.sharding import PartitionSpec as P
 
 QH = 32
@@ -119,6 +123,390 @@
     return (widened + routed).astype(jnp.bfloat16)
 
 
+GATE_SLOTS = 5
+DOWN_SLOTS = 3
+MESH = pl.DeviceIdType.MESH
+
+
+def layer_kernel(
+    roles,
+    att_ref,
+    small_ref,
+    proj_ref,
+    gain_ref,
+    wg_ref,
+    wu_ref,
+    wd_ref,
+    out_ref,
+    att_all,
+    small_all,
+    hid_all,
+    normed,
+    activation,
+    total,
+    part,
+    got_core,
+    got_row,
+    got_col,
+    gate_up,
+    down,
+    gate_sem,
+    down_sem,
+    att_send,
+    att_recv,
+    small_send,
+    small_recv,
+    hid_send,
+    hid_recv,
+    core_send,
+    core_recv,
+    row_send,
+    row_recv,
+    col_send,
+    col_recv,
+):
+    devs = 4
+    devices = devs * roles
+    grp = lax.axis_index("grp")
+    dev = lax.axis_index("dev")
+    role = lax.axis_index("role")
+    me = dev * roles + role
+    sibling = dev + 1 - 2 * lax.rem(dev, 2)
+    across = lax.rem(dev + 2, 4)
+    diagonal = lax.rem(sibling + 2, 4)
+    slots, width, half = wg_ref.shape
+    pairs = slots // 2
+    columns = proj_ref.shape[1]
+    rows = 8
+    tokens = devices * rows
+    folded = width // 2
+
+    def gate_copies(s, slot):
+        return (
+            pltpu.make_async_copy(
+                wg_ref.at[s], gate_up.at[slot, :, pl.ds(0, half)], gate_sem.at[slot, 0]
+            ),
+            pltpu.make_async_copy(
+                wu_ref.at[s], gate_up.at[slot, :, pl.ds(half, half)], gate_sem.at[slot, 1]
+            ),
+        )
+
+    def down_copy(e, slot):
+        return pltpu.make_async_copy(
+            wd_ref.at[pl.ds(2 * e, 2)], down.at[slot], down_sem.at[slot]
+        )
+
+    for s in range(min(GATE_SLOTS, slots)):
+        for copy in gate_copies(s, s):
+            copy.start()
+        if s % 2 == 1 and s // 2 < min(DOWN_SLOTS, pairs):
+            down_copy(s // 2, s // 2).start()
+    for e in range(min(GATE_SLOTS, slots) // 2, min(DOWN_SLOTS, pairs)):
+        down_copy(e, e).start()
+
+    def coords(k):
+        other = lax.rem(me + k, devices)
+        return other, (grp, other // roles, lax.rem(other, roles))
+
+    barrier = pltpu.get_barrier_semaphore()
+    for k in range(1, devices):
+        pl.semaphore_signal(barrier, inc=1, device_id=coords(k)[1], device_id_type=MESH)
+    pl.semaphore_wait(barrier, devices - 1)
+
+    def send(src, dst, send_sem, recv_sem, target):
+        copy = pltpu.make_async_remote_copy(
+            src_ref=src,
+            dst_ref=dst,
+            send_sem=send_sem,
+            recv_sem=recv_sem,
+            device_id=target,
+            device_id_type=MESH,
+        )
+        copy.start()
+        return copy
+
+    def gather(buf, send_sem, recv_sem, used):
+        started = []
+
+        def push(rank, target):
+            started.append(
+                send(
+                    buf.at[rank],
+                    buf.at[rank],
+                    send_sem.at[len(started)],
+                    recv_sem.at[rank],
+                    target,
+                )
+            )
+
+        def arrived(rank):
+            pltpu.make_async_copy(buf.at[rank], buf.at[rank], recv_sem.at[rank]).wait()
+
+        for k in range(1, roles):
+            push(me, (grp, dev, lax.rem(role + k, roles)))
+        push(me, (grp, across, role))
+        push(me, (grp, sibling, role))
+        used(me)
+        for k in range(1, roles):
+            rank = dev * roles + lax.rem(role + roles - k, roles)
+            arrived(rank)
+            push(rank, (grp, across, role))
+            push(rank, (grp, sibling, role))
+            used(rank)
+        for k in range(roles):
+            rank = across * roles + lax.rem(role + roles - k, roles)
+            arrived(rank)
+            push(rank, (grp, sibling, role))
+            used(rank)
+        for owner in (sibling, diagonal):
+            for k in range(roles):
+                rank = owner * roles + lax.rem(role + roles - k, roles)
+                arrived(rank)
+                used(rank)
+        return started
+
+    att_all[me] = att_ref[...]
+    small_all[me] = small_ref[me]
+    small_copies = []
+    for k in range(1, devices):
+        other, target = coords(k)
+        small_copies.append(
+            send(
+                small_ref.at[other],
+                small_all.at[me],
+                small_send.at[k],
+                small_recv.at[k],
+                target,
+            )
+        )
+    started = gather(att_all, att_send, att_recv, lambda rank: None)
+    for copy in small_copies:
+        copy.wait_recv()
+
+    left = att_all[...].reshape(devices * 16, folded)
+    low = jnp.dot(left, proj_ref[:folded, :], preferred_element_type=jnp.float32)
+    high = jnp.dot(left, proj_ref[folded:, :], preferred_element_type=jnp.float32)
+    low = low.reshape(devices, 16, columns)[:, :rows]
+    high = high.reshape(devices, 16, columns)[:, rows:]
+    hidden = small_all[:, :, :columns] + (low + high)
+    hid_all[me] = hidden.reshape(tokens, columns).astype(jnp.bfloat16)
+    weights = small_all[:, :, columns:].reshape(tokens, 128)
+    lane = lax.broadcasted_iota(jnp.int32, (tokens, 128), 1)
+
+    squares = [jnp.zeros((tokens, columns), jnp.float32)]
+
+    def add_squares(rank):
+        block = hid_all[rank].astype(jnp.float32)
+        squares[0] = squares[0] + block * block
+
+    started += gather(hid_all, hid_send, hid_recv, add_squares)
+    mean = jnp.sum(squares[0], axis=1, keepdims=True) / width
+    scale = lax.rsqrt(mean + 1e-06)
+
+    for k in range(devices):
+        cols = slice(k * columns, (k + 1) * columns)
+        block = hid_all[k].astype(jnp.float32)
+        normed[:, cols] = (block * scale * gain_ref[:, cols]).astype(jnp.bfloat16)
+
+    def one_pair(e, carry):
+        expert = me * pairs + e
+        weight = jnp.sum(jnp.where(lane == expert, weights, 0.0), axis=1, keepdims=True)
+
+        def one_half(j, inner):
+            s = 2 * e + j
+            slot = lax.rem(s, GATE_SLOTS)
+            for copy in gate_copies(s, slot):
+                copy.wait()
+            both = jnp.dot(normed[...], gate_up[slot], preferred_element_type=jnp.float32)
+            gate = both[:, :half]
+            value = gate / (1.0 + jnp.exp(-gate)) * both[:, half:] * weight
+            activation[j] = value.astype(jnp.bfloat16)
+
+            @pl.when(s + GATE_SLOTS < slots)
+            def _():
+                for copy in gate_copies(s + GATE_SLOTS, slot):
+                    copy.start()
+
+            return inner
+
+        lax.fori_loop(0, 2, one_half, 0)
+        slot = lax.rem(e, DOWN_SLOTS)
+        down_copy(e, slot).wait()
+        act = jnp.concatenate([activation[0], activation[1]], axis=1)
+
+        def one_chunk(c, inner):
+            cols = pl.ds(pl.multiple_of(c * 512, 512), 512)
+            piece = jnp.dot(
+                act,
+                down[slot, :, :, cols].reshape(2 * half, 512),
+                preferred_element_type=jnp.float32,
+            )
+
+            @pl.when(e == 0)
+            def _():
+                total[:, cols] = piece
+
+            @pl.when(e > 0)
+            def _():
+                total[:, cols] = total[:, cols] + piece
+
+            return inner
+
+        lax.fori_loop(0, width // 512, one_chunk, 0)
+
+        @pl.when(e + DOWN_SLOTS < pairs)
+        def _():
+            down_copy(e + DOWN_SLOTS, slot).start()
+
+        return carry
+
+    lax.fori_loop(0, pairs, one_pair, 0)
+
+    for c in range(folded // 256):
+        lower = total[:, c * 256 : (c + 1) * 256].reshape(devs, roles, rows, 256)
+        upper = total[:, folded + c * 256 : folded + (c + 1) * 256].reshape(
+            devs, roles, rows, 256
+        )
+        part[:, :, :, c * 256 : (c + 1) * 256] = jnp.concatenate(
+            [lower, upper], axis=2
+        ).astype(jnp.bfloat16)
+
+    first = send(
+        part.at[diagonal], got_core.at[1], core_send.at[1], core_recv.at[1], (grp, sibling, role)
+    )
+    second = send(
+        part.at[sibling], got_core.at[0], core_send.at[0], core_recv.at[0], (grp, sibling, role)
+    )
+    started += [first, second]
+    first.wait_recv()
+    part[across] = (
+        part[across].astype(jnp.float32) + got_core[1].astype(jnp.float32)
+    ).astype(jnp.bfloat16)
+    crossing = send(
+        part.at[across], got_row, row_send.at[0], row_recv.at[0], (grp, across, role)
+    )
+    started.append(crossing)
+    second.wait_recv()
+    crossing.wait_recv()
+    part[dev] = (
+        part[dev].astype(jnp.float32)
+        + got_core[0].astype(jnp.float32)
+        + got_row[...].astype(jnp.float32)
+    ).astype(jnp.bfloat16)
+    along = []
+    for k in range(1, roles):
+        other = lax.rem(role + k, roles)
+        along.append(
+            send(
+                part.at[dev, other],
+                got_col.at[k - 1],
+                col_send.at[k - 1],
+                col_recv.at[k - 1],
+                (grp, dev, other),
+            )
+        )
+    started += along
+
+    mine = (
+        lax.broadcasted_iota(jnp.int32, (rows, tokens), 1)
+        == lax.broadcasted_iota(jnp.int32, (rows, tokens), 0) + me * rows
+    ).astype(jnp.bfloat16)
+    own = [
+        jnp.dot(mine, hid_all[k], preferred_element_type=jnp.float32) for k in range(devices)
+    ]
+    for copy in along:
+        copy.wait_recv()
+    routed = part[dev, role].astype(jnp.float32)
+    for k in range(roles - 1):
+        routed = routed + got_col[k].astype(jnp.float32)
+    for k in range(devices):
+        at = k * columns
+        piece = routed[:rows, at : at + columns] if at < folded else (
+            routed[rows:, at - folded : at - folded + columns]
+        )
+        out_ref[:, at : at + columns] = (own[k] + piece).astype(jnp.bfloat16)
+    for copy in started:
+        copy.wait_send()
+    for copy in small_copies:
+        copy.wait_send()
+
+
+def fused_body(
+    roles,
+    queries,
+    key_cache,
+    value_cache,
+    new_key,
+    new_value,
+    lengths,
+    residual,
+    out_proj,
+    norm_gain,
+    expert_ids,
+    gate_weights,
+    w_gate,
+    w_up,
+    w_down,
+):
+    devices = 4 * roles
+    count, width = residual.shape
+    columns = out_proj.shape[1]
+    half = w_gate.shape[2]
+    attended = attend_rows(queries, key_cache, value_cache, new_key, new_value, lengths)
+    attended = attended.reshape(count, 2, width // 2).swapaxes(0, 1).reshape(16, width // 2)
+    named = expert_ids[:, :, None] == jnp.arange(128, dtype=jnp.int32)[None, None, :]
+    combine = jnp.sum(jnp.where(named, gate_weights[:, :, None], 0.0), axis=1)
+    small = jnp.concatenate(
+        [
+            residual.astype(jnp.float32).reshape(count, devices, columns).swapaxes(0, 1),
+            jnp.broadcast_to(combine[None], (devices, count, 128)),
+        ],
+        axis=2,
+    )
+    tokens = devices * count
+    dma = pltpu.SemaphoreType.DMA
+    vmem = pl.BlockSpec(memory_space=pltpu.VMEM)
+    hbm = pl.BlockSpec(memory_space=pl.ANY)
+    bf16 = jnp.bfloat16
+    return pl.pallas_call(
+        functools.partial(layer_kernel, roles),
+        out_shape=jax.ShapeDtypeStruct((count, width), bf16),
+        in_specs=[vmem] * 4 + [hbm] * 3,
+        out_specs=vmem,
+        scratch_shapes=[
+            pltpu.VMEM((devices, 16, width // 2), bf16),
+            pltpu.VMEM((devices, count, columns + 128), jnp.float32),
+            pltpu.VMEM((devices, tokens, columns), bf16),
+            pltpu.VMEM((tokens, width), bf16),
+            pltpu.VMEM((2, tokens, half), bf16),
+            pltpu.VMEM((tokens, width), jnp.float32),
+            pltpu.VMEM((4, roles, 16, width // 2), bf16),
+            pltpu.VMEM((2, roles, 16, width // 2), bf16),
+            pltpu.VMEM((roles, 16, width // 2), bf16),
+            pltpu.VMEM((roles - 1, 16, width // 2), bf16),
+            pltpu.VMEM((GATE_SLOTS, width, 2 * half), bf16),
+            pltpu.VMEM((DOWN_SLOTS, 2, half, width), bf16),
+            dma((GATE_SLOTS, 2)),
+            dma((DOWN_SLOTS,)),
+            dma((devices - 1,)),
+            dma((devices,)),
+            dma((devices,)),
+            dma((devices,)),
+            dma((devices - 1,)),
+            dma((devices,)),
+            dma((2,)),
+            dma((2,)),
+            dma((1,)),
+            dma((1,)),
+            dma((roles - 1,)),
+            dma((roles - 1,)),
+        ],
+        compiler_params=pltpu.CompilerParams(
+            collective_id=0, has_side_effects=True, vmem_limit_bytes=62 * 1024 * 1024
+        ),
+    )(attended, small, out_proj, norm_gain.reshape(1, width), w_gate, w_up, w_down)
+
+
 def solution(mesh):
     placed = (
         P(("grp", "dev", "role"), None),
@@ -136,6 +524,9 @@
         P(("dev", "role"), None, None),
         P(("dev", "role"), None, None),
     )
+    devs, roles = mesh.shape["dev"], mesh.shape["role"]
+    fits = devs == 4 and roles == 4
+    chosen = functools.partial(fused_body, roles) if fits else body
     return jax.shard_map(
-        body, mesh=mesh, in_specs=placed, out_specs=P(("grp", "dev", "role"), None), check_vma=False
-    )
+        chosen, mesh=mesh, in_specs=placed, out_specs=P(("grp", "dev", "role"), None), check_vma=False
+    )

time: 233 us -> 81.3 us (0.35)
  waiting for transfers between devices: 96.5 us -> 0 us
  Pallas kernels: 0 us -> 70.3 us
  blocking collectives: 52.5 us -> 0 us
  matrix products: 42.5 us -> 4.23 us
  between operations: 13.5 us -> 0.05 us
  local copies, waits for them, and re-layouts: 12.9 us -> 2.17 us
  starting transfers between devices: 7.69 us -> 0 us
  other arithmetic: 6.58 us -> 4.11 us
    pallas_call x0 -> x1, Pallas kernels: none -> 70.3 us  [fused_body(): pl.pallas_call(functools.partial(layer_kernel, roles), out_shape=jax.Shap...]
    all_to_all x2 -> x0, waiting for transfers between devices: 56.2 us -> none  [the longest x1 49 us: body(): lax.all_to_all(produced.astype(jnp.bfloat16), ('dev', 'role'), split_axis...]
    all_to_all x1 -> x0, blocking collectives: 52.5 us -> none  [body(): lax.all_to_all(outgoing, ('dev', 'role'), split_axis=0, concat_axis=0, ti...]
    all_gather x1 -> x0, waiting for transfers between devices: 40.3 us -> none  [body(): lax.all_gather(attended, ('dev', 'role'), axis=0, tiled=True)]
    dot_general x6 -> x0, matrix products: 37.9 us -> none  [the longest x1 21.2 us: expert_work(): jnp.einsum('psch,shd->pscd', activation, w_down, preferred_element_type=j...]
    all_to_all x2 -> x0, starting transfers between devices: 7.69 us -> none  [the longest x1 4.07 us: body(): lax.all_to_all(produced.astype(jnp.bfloat16), ('dev', 'role'), split_axis...]
    convert_element_type x1 -> x2, local copies, waits for them, and re-layouts: 5.07 us -> 0.68 us  [attend_rows(): return combined.reshape(count, QH * HD).astype(jnp.bfloat16)]
    reshape x1 -> x0, local copies, waits for them, and re-layouts: 3.81 us -> none  [body(): expert_out.reshape(EXPERTS * capacity, width)]
  transfers between devices with their start and end apart: 3 -> 0, of which waited for: 3 -> 0; matrix products, arithmetic and copies ran while one was open for 0% -> 0% of each run, Pallas kernels for 0% -> 0%
where the time goes in v1:
time: 81.3 us; the launch traced here: 80.9 us
  Pallas kernels  70.3 us (86%)
  matrix products  4.23 us (5%)
  other arithmetic  4.11 us (5%)
  local copies, waits for them, and re-layouts  2.17 us (3%)
    pallas_call x1, Pallas kernels, fused_body(): pl.pallas_call(functools.partial(layer_kernel, roles), out_shape=jax.Shap...  70.3 us
    dot_general x1, matrix products, attend_rows(): jnp.einsum('rkgt,rtkd->rkgd', probs, cached_values, preferred_element_typ...  1.67 us

profile of v1, /device:TPU:0, one launch (start us, length us, event | category | flops | bytes accessed | tf_op | source)
XLA Modules:
  0.0 80.9 jit_solution(11510959852503439388)
XLA Ops:
  0.0 0.0 copy-start
  0.0 0.8 %iota_compare_fusion.1 = pred[8,128]{1,0:T(8,128)(4,1)S(1)} fusion(s32[8]{0:T(128)} %param.19), kind=kLoop, calls=%fused_computation.27 | loop fusion | flops 1024 | bytes 1056 | tf_op jit(solution)/shard_map/lt | solution.py:34
  0.8 0.8 select_reduce_fusion
  1.6 1.0 %fusion.9 = f32[8,4,1,8]{3,2,1,0:T(1,128)S(1)} fusion(bf16[8,4,8,128]{3,0,2,1:T(8,128)(2,1)} %bitcast.39, bf16[8,4,128,1]{2,0,1,3:T(8,128)(2,1)} %bitcast.44), kind=kOutput, calls=%fused_computation.16 | convolution fusion | flops 65536 | bytes 74752 | tf_op jit(solution)/shard_map/rkgd,rkd->rkg/dot_general | solution.py:31
  2.6 0.7 bitcast_convert_fusion
  3.3 0.9 %convert_bitcast_fusion = f32[16,8,256]{2,1,0:T(8,128)S(1)} fusion(bf16[8,16,256]{2,0,1:T(8,128)(2,1)} %bitcast.38), kind=kLoop, calls=%fused_computation.9 | loop fusion | flops 32768 | bytes 196608 | tf_op jit(solution)/shard_map/transpose | solution.py:461
  4.2 0.7 pad_maximum_fusion.small_ref
  4.9 0.0 copy-done
  4.9 1.6 %fusion.15 = (f32[8,4,8]{2,1,0:T(4,128)S(1)}, f32[8,4,8,128]{3,2,1,0:T(8,128)S(1)}) fusion(bf16[8,4,8,128]{3,0,2,1:T(8,128)(2,1)} %bitcast.40, pred[8,128]{1,0:T(8,128)(4,1)S(1)} %iota_compare_fusion.1, bf16[8,128,512]{2,1,0:T(8,128)(2,1)S(1)} %copy-done), kind=kOutput, calls=%fused_computation.29 | convolution fusion | flops 8486656 | bytes 1247232 | tf_op jit(solution)/shard_map/rkgd,rtkd->rkgt/dot_general | solution.py:27
  6.5 0.2 fusion.6
  6.7 1.7 %fusion.1 = bf16[8,4,8,128]{3,2,1,0:T(8,128)(2,1)S(1)} fusion(f32[8,4,8,128]{3,2,1,0:T(8,128)S(1)} %get-tuple-element.8, f32[8,4,128]{2,1,0:T(4,128)S(1)} %copy.23, f32[8,4,8]{2,1,0:T(4,128)S(1)} %get-tuple-element.6, f32[8,4,8]{2,1,0:T(4,128)S(1)} %get-tuple-element.5, f32[8,4,8]{2,1,0:T(4,128)S(1)} %multiply_maximum_fusion, bf16[8,128,512]{2,1,0:T(8,128)(2,1)} %param.16), kind=kOutput, calls=%fused_computation.3 | convolution fusion | flops 8585216 | bytes 1264640 | tf_op jit(solution)/shard_map/rkgt,rtkd->rkgd/dot_general | solution.py:42
  8.4 0.7 copy.48
  9.1 70.3 %shard_map.136 = bf16[8,4096]{1,0:T(8,128)(2,1)} custom-call(bf16[16,2048]{1,0:T(8,128)(2,1)} %bitcast.37, f32[16,8,384]{2,1,0:T(8,128)} %pad_maximum_fusion.small_ref, bf16[4096,256]{1,0:T(8,128)(2,1)} %proj_ref.1, f32[1,4096]{1,0:T(1,128)} %bitcast.43, bf16[8,4096,384]{2,1,0:T(8,128)(2,1)} %wg_ref.1, bf16[8,4096,384]{2,1,0:T(8,128)(2,1)} %wu_ref.1, ...), custom_call_target="tpu_custom_call" | custom-call | tf_op jit(solution)/shard_map/pallas_call | solution.py:471
  79.4 1.5 %copy.50 = bf16[8,4096]{1,0:T(8,128)(2,1)} copy(bf16[8,4096]{1,0:T(8,128)(2,1)} %shard_map.136) | data formatting | bytes 131072
  (5 shorter events, 0.1 us)
Async XLA Ops:
  0.0 4.9 %copy-start = (bf16[8,128,512]{2,1,0:T(8,128)(2,1)S(1)}, bf16[8,128,512]{2,1,0:T(8,128)(2,1)}, u32[]{:S(2)}) copy-start(bf16[8,128,512]{2,1,0:T(8,128)(2,1)} %param.15) | copy-start | bytes 3145732

commit v2 on v1

--- a/solution.py
+++ b/solution.py
@@ -125,13 +125,16 @@
 
 GATE_SLOTS = 5
 DOWN_SLOTS = 3
+CHUNKS = 4
 MESH = pl.DeviceIdType.MESH
 
 
 def layer_kernel(
     roles,
     att_ref,
-    small_ref,
+    residual_ref,
+    ids_ref,
+    mix_ref,
     proj_ref,
     gain_ref,
     wg_ref,
@@ -139,11 +142,12 @@
     wd_ref,
     out_ref,
     att_all,
+    small_out,
     small_all,
+    own,
     hid_all,
     normed,
     activation,
-    total,
     part,
     got_core,
     got_row,
@@ -180,6 +184,7 @@
     rows = 8
     tokens = devices * rows
     folded = width // 2
+    span = folded // CHUNKS
 
     def gate_copies(s, slot):
         return (
@@ -191,18 +196,23 @@
             ),
         )
 
-    def down_copy(e, slot):
-        return pltpu.make_async_copy(
-            wd_ref.at[pl.ds(2 * e, 2)], down.at[slot], down_sem.at[slot]
-        )
+    def down_copies(c):
+        slot = c % DOWN_SLOTS
+        return [
+            pltpu.make_async_copy(
+                wd_ref.at[:, :, pl.ds(j * folded + c * span, span)],
+                down.at[slot, j],
+                down_sem.at[slot, j],
+            )
+            for j in range(2)
+        ]
 
     for s in range(min(GATE_SLOTS, slots)):
         for copy in gate_copies(s, s):
             copy.start()
-        if s % 2 == 1 and s // 2 < min(DOWN_SLOTS, pairs):
-            down_copy(s // 2, s // 2).start()
-    for e in range(min(GATE_SLOTS, slots) // 2, min(DOWN_SLOTS, pairs)):
-        down_copy(e, e).start()
+    for c in range(DOWN_SLOTS):
+        for copy in down_copies(c):
+            copy.start()
 
     def coords(k):
         other = lax.rem(me + k, devices)
@@ -211,6 +221,18 @@
     barrier = pltpu.get_barrier_semaphore()
     for k in range(1, devices):
         pl.semaphore_signal(barrier, inc=1, device_id=coords(k)[1], device_id_type=MESH)
+
+    combine = jnp.zeros((rows, 128), jnp.float32)
+    column = lax.broadcasted_iota(jnp.int32, (rows, 128), 1)
+    for k in range(TOP):
+        combine += jnp.where(column == ids_ref[:, k : k + 1], mix_ref[:, k : k + 1], 0.0)
+    for k in range(devices):
+        small_out[k, :, :columns] = residual_ref[:, k * columns : (k + 1) * columns].astype(
+            jnp.float32
+        )
+        small_out[k, :, columns:] = combine
+    att_all[me] = att_ref[...]
+    small_all[me] = small_out[me]
     pl.semaphore_wait(barrier, devices - 1)
 
     def send(src, dst, send_sem, recv_sem, target):
@@ -265,14 +287,12 @@
                 used(rank)
         return started
 
-    att_all[me] = att_ref[...]
-    small_all[me] = small_ref[me]
     small_copies = []
     for k in range(1, devices):
         other, target = coords(k)
         small_copies.append(
             send(
-                small_ref.at[other],
+                small_out.at[other],
                 small_all.at[me],
                 small_send.at[k],
                 small_recv.at[k],
@@ -308,123 +328,119 @@
         block = hid_all[k].astype(jnp.float32)
         normed[:, cols] = (block * scale * gain_ref[:, cols]).astype(jnp.bfloat16)
 
-    def one_pair(e, carry):
-        expert = me * pairs + e
+    def one_half(s, carry):
+        expert = me * pairs + s // 2
         weight = jnp.sum(jnp.where(lane == expert, weights, 0.0), axis=1, keepdims=True)
-
-        def one_half(j, inner):
-            s = 2 * e + j
-            slot = lax.rem(s, GATE_SLOTS)
-            for copy in gate_copies(s, slot):
-                copy.wait()
-            both = jnp.dot(normed[...], gate_up[slot], preferred_element_type=jnp.float32)
-            gate = both[:, :half]
-            value = gate / (1.0 + jnp.exp(-gate)) * both[:, half:] * weight
-            activation[j] = value.astype(jnp.bfloat16)
-
-            @pl.when(s + GATE_SLOTS < slots)
-            def _():
-                for copy in gate_copies(s + GATE_SLOTS, slot):
-                    copy.start()
-
-            return inner
-
-        lax.fori_loop(0, 2, one_half, 0)
-        slot = lax.rem(e, DOWN_SLOTS)
-        down_copy(e, slot).wait()
-        act = jnp.concatenate([activation[0], activation[1]], axis=1)
-
-        def one_chunk(c, inner):
-            cols = pl.ds(pl.multiple_of(c * 512, 512), 512)
-            piece = jnp.dot(
-                act,
-                down[slot, :, :, cols].reshape(2 * half, 512),
+        slot = lax.rem(s, GATE_SLOTS)
+        for copy in gate_copies(s, slot):
+            copy.wait()
+        both = jnp.dot(normed[...], gate_up[slot], preferred_element_type=jnp.float32)
+        gate = both[:, :half]
+        value = gate / (1.0 + jnp.exp(-gate)) * both[:, half:] * weight
+        activation[:, pl.ds(pl.multiple_of(s * half, 128), half)] = value.astype(jnp.bfloat16)
+
+        @pl.when(s + GATE_SLOTS < slots)
+        def _():
+            for copy in gate_copies(s + GATE_SLOTS, slot):
+                copy.start()
+
+        return carry
+
+    lax.fori_loop(0, slots, one_half, 0)
+
+    to_core, to_row, to_col = {}, {}, {}
+
+    def share(c):
+        slot = c % DOWN_SLOTS
+        for copy in down_copies(c):
+            copy.wait()
+        lower, upper = [
+            jnp.dot(
+                activation[...],
+                down[slot, j].reshape(slots * half, span),
                 preferred_element_type=jnp.float32,
+            ).reshape(devs, roles, rows, span)
+            for j in range(2)
+        ]
+        if c + DOWN_SLOTS < CHUNKS:
+            for copy in down_copies(c + DOWN_SLOTS):
+                copy.start()
+        part[c] = jnp.concatenate([lower, upper], axis=2).astype(jnp.bfloat16)
+        to_core[c] = [
+            send(
+                part.at[c, owner],
+                got_core.at[c, j],
+                core_send.at[c, j],
+                core_recv.at[c, j],
+                (grp, sibling, role),
             )
-
-            @pl.when(e == 0)
-            def _():
-                total[:, cols] = piece
-
-            @pl.when(e > 0)
-            def _():
-                total[:, cols] = total[:, cols] + piece
-
-            return inner
-
-        lax.fori_loop(0, width // 512, one_chunk, 0)
-
-        @pl.when(e + DOWN_SLOTS < pairs)
-        def _():
-            down_copy(e + DOWN_SLOTS, slot).start()
-
-        return carry
-
-    lax.fori_loop(0, pairs, one_pair, 0)
-
-    for c in range(folded // 256):
-        lower = total[:, c * 256 : (c + 1) * 256].reshape(devs, roles, rows, 256)
-        upper = total[:, folded + c * 256 : folded + (c + 1) * 256].reshape(
-            devs, roles, rows, 256
+            for j, owner in ((1, diagonal), (0, sibling))
+        ]
+
+    def cross(c):
+        to_core[c][0].wait_recv()
+        part[c, across] = (
+            part[c, across].astype(jnp.float32) + got_core[c, 1].astype(jnp.float32)
+        ).astype(jnp.bfloat16)
+        to_row[c] = send(
+            part.at[c, across],
+            got_row.at[c],
+            row_send.at[c],
+            row_recv.at[c],
+            (grp, across, role),
         )
-        part[:, :, :, c * 256 : (c + 1) * 256] = jnp.concatenate(
-            [lower, upper], axis=2
+
+    def finish(c):
+        to_core[c][1].wait_recv()
+        to_row[c].wait_recv()
+        part[c, dev] = (
+            part[c, dev].astype(jnp.float32)
+            + got_core[c, 0].astype(jnp.float32)
+            + got_row[c].astype(jnp.float32)
         ).astype(jnp.bfloat16)
-
-    first = send(
-        part.at[diagonal], got_core.at[1], core_send.at[1], core_recv.at[1], (grp, sibling, role)
-    )
-    second = send(
-        part.at[sibling], got_core.at[0], core_send.at[0], core_recv.at[0], (grp, sibling, role)
-    )
-    started += [first, second]
-    first.wait_recv()
-    part[across] = (
-        part[across].astype(jnp.float32) + got_core[1].astype(jnp.float32)
-    ).astype(jnp.bfloat16)
-    crossing = send(
-        part.at[across], got_row, row_send.at[0], row_recv.at[0], (grp, across, role)
-    )
-    started.append(crossing)
-    second.wait_recv()
-    crossing.wait_recv()
-    part[dev] = (
-        part[dev].astype(jnp.float32)
-        + got_core[0].astype(jnp.float32)
-        + got_row[...].astype(jnp.float32)
-    ).astype(jnp.bfloat16)
-    along = []
-    for k in range(1, roles):
-        other = lax.rem(role + k, roles)
-        along.append(
-            send(
-                part.at[dev, other],
-                got_col.at[k - 1],
-                col_send.at[k - 1],
-                col_recv.at[k - 1],
-                (grp, dev, other),
+        to_col[c] = []
+        for k in range(1, roles):
+            other = lax.rem(role + k, roles)
+            to_col[c].append(
+                send(
+                    part.at[c, dev, other],
+                    got_col.at[c, k - 1],
+                    col_send.at[c, k - 1],
+                    col_recv.at[c, k - 1],
+                    (grp, dev, other),
+                )
             )
-        )
-    started += along
+
+    for c in range(CHUNKS):
+        share(c)
+        if c >= 1:
+            cross(c - 1)
+        if c >= 2:
+            finish(c - 2)
+    cross(CHUNKS - 1)
+    finish(CHUNKS - 2)
 
     mine = (
         lax.broadcasted_iota(jnp.int32, (rows, tokens), 1)
         == lax.broadcasted_iota(jnp.int32, (rows, tokens), 0) + me * rows
     ).astype(jnp.bfloat16)
-    own = [
-        jnp.dot(mine, hid_all[k], preferred_element_type=jnp.float32) for k in range(devices)
-    ]
-    for copy in along:
-        copy.wait_recv()
-    routed = part[dev, role].astype(jnp.float32)
-    for k in range(roles - 1):
-        routed = routed + got_col[k].astype(jnp.float32)
     for k in range(devices):
-        at = k * columns
-        piece = routed[:rows, at : at + columns] if at < folded else (
-            routed[rows:, at - folded : at - folded + columns]
+        own[:, k * columns : (k + 1) * columns] = jnp.dot(
+            mine, hid_all[k], preferred_element_type=jnp.float32
         )
-        out_ref[:, at : at + columns] = (own[k] + piece).astype(jnp.bfloat16)
+    finish(CHUNKS - 1)
+    for c in range(CHUNKS):
+        for copy in to_col[c]:
+            copy.wait_recv()
+        routed = part[c, dev, role].astype(jnp.float32)
+        for k in range(roles - 1):
+            routed = routed + got_col[c, k].astype(jnp.float32)
+        for j in range(2):
+            cols = slice(j * folded + c * span, j * folded + (c + 1) * span)
+            out_ref[:, cols] = (own[:, cols] + routed[j * rows : (j + 1) * rows]).astype(
+                jnp.bfloat16
+            )
+        started += to_core[c] + [to_row[c]] + to_col[c]
     for copy in started:
         copy.wait_send()
     for copy in small_copies:
@@ -451,18 +467,10 @@
     devices = 4 * roles
     count, width = residual.shape
     columns = out_proj.shape[1]
-    half = w_gate.shape[2]
+    slots, half = w_gate.shape[0], w_gate.shape[2]
+    span = width // 2 // CHUNKS
     attended = attend_rows(queries, key_cache, value_cache, new_key, new_value, lengths)
     attended = attended.reshape(count, 2, width // 2).swapaxes(0, 1).reshape(16, width // 2)
-    named = expert_ids[:, :, None] == jnp.arange(128, dtype=jnp.int32)[None, None, :]
-    combine = jnp.sum(jnp.where(named, gate_weights[:, :, None], 0.0), axis=1)
-    small = jnp.concatenate(
-        [
-            residual.astype(jnp.float32).reshape(count, devices, columns).swapaxes(0, 1),
-            jnp.broadcast_to(combine[None], (devices, count, 128)),
-        ],
-        axis=2,
-    )
     tokens = devices * count
     dma = pltpu.SemaphoreType.DMA
     vmem = pl.BlockSpec(memory_space=pltpu.VMEM)
@@ -471,40 +479,51 @@
     return pl.pallas_call(
         functools.partial(layer_kernel, roles),
         out_shape=jax.ShapeDtypeStruct((count, width), bf16),
-        in_specs=[vmem] * 4 + [hbm] * 3,
+        in_specs=[vmem] * 6 + [hbm] * 3,
         out_specs=vmem,
         scratch_shapes=[
             pltpu.VMEM((devices, 16, width // 2), bf16),
             pltpu.VMEM((devices, count, columns + 128), jnp.float32),
+            pltpu.VMEM((devices, count, columns + 128), jnp.float32),
+            pltpu.VMEM((count, width), jnp.float32),
             pltpu.VMEM((devices, tokens, columns), bf16),
             pltpu.VMEM((tokens, width), bf16),
-            pltpu.VMEM((2, tokens, half), bf16),
-            pltpu.VMEM((tokens, width), jnp.float32),
-            pltpu.VMEM((4, roles, 16, width // 2), bf16),
-            pltpu.VMEM((2, roles, 16, width // 2), bf16),
-            pltpu.VMEM((roles, 16, width // 2), bf16),
-            pltpu.VMEM((roles - 1, 16, width // 2), bf16),
+            pltpu.VMEM((tokens, slots * half), bf16),
+            pltpu.VMEM((CHUNKS, 4, roles, 16, span), bf16),
+            pltpu.VMEM((CHUNKS, 2, roles, 16, span), bf16),
+            pltpu.VMEM((CHUNKS, roles, 16, span), bf16),
+            pltpu.VMEM((CHUNKS, roles - 1, 16, span), bf16),
             pltpu.VMEM((GATE_SLOTS, width, 2 * half), bf16),
-            pltpu.VMEM((DOWN_SLOTS, 2, half, width), bf16),
+            pltpu.VMEM((DOWN_SLOTS, 2, slots, half, span), bf16),
             dma((GATE_SLOTS, 2)),
-            dma((DOWN_SLOTS,)),
+            dma((DOWN_SLOTS, 2)),
             dma((devices - 1,)),
             dma((devices,)),
             dma((devices,)),
             dma((devices,)),
             dma((devices - 1,)),
             dma((devices,)),
-            dma((2,)),
-            dma((2,)),
-            dma((1,)),
-            dma((1,)),
-            dma((roles - 1,)),
-            dma((roles - 1,)),
+            dma((CHUNKS, 2)),
+            dma((CHUNKS, 2)),
+            dma((CHUNKS,)),
+            dma((CHUNKS,)),
+            dma((CHUNKS, roles - 1)),
+            dma((CHUNKS, roles - 1)),
         ],
         compiler_params=pltpu.CompilerParams(
             collective_id=0, has_side_effects=True, vmem_limit_bytes=62 * 1024 * 1024
         ),
-    )(attended, small, out_proj, norm_gain.reshape(1, width), w_gate, w_up, w_down)
+    )(
+        attended,
+        residual,
+        expert_ids,
+        gate_weights,
+        out_proj,
+        norm_gain.reshape(1, width),
+        w_gate,
+        w_up,
+        w_down,
+    )
 
 
 def solution(mesh):

time: 81.3 us -> 71.1 us (0.87)
  Pallas kernels: 70.3 us -> 62.6 us
  other arithmetic: 4.11 us -> 1.78 us
    pallas_call x1, Pallas kernels: 70.3 us -> 62.6 us  [fused_body(): pl.pallas_call(functools.partial(layer_kernel, roles), out_shape=jax.Shap...]
    transpose x1 -> x0, other arithmetic: 0.85 us -> none  [fused_body(): residual.astype(jnp.float32).reshape(count, devices, columns).swapaxes(0, 1)]
where the time goes in v2:
time: 71.1 us; the launch traced here: 70.8 us
  Pallas kernels  62.6 us (88%)
  matrix products  4.23 us (6%)
  local copies, waits for them, and re-layouts  2.17 us (3%)
  other arithmetic  1.78 us (3%)
    pallas_call x1, Pallas kernels, fused_body(): pl.pallas_call(functools.partial(layer_kernel, roles), out_shape=jax.Shap...  62.6 us
    dot_general x1, matrix products, attend_rows(): jnp.einsum('rkgt,rtkd->rkgd', probs, cached_values, preferred_element_typ...  1.67 us
    dot_general x1, matrix products, attend_rows(): jnp.einsum('rkgd,rtkd->rkgt', grouped, cached_keys, preferred_element_typ...  1.56 us
    unnamed x3, local copies, waits for them, and re-layouts  1.48 us

profile of v2, /device:TPU:0, one launch (start us, length us, event | category | flops | bytes accessed | tf_op | source)
XLA Modules:
  0.0 70.8 jit_solution(6367484911229360811)
XLA Ops:
  0.0 0.0 copy-start
  0.0 0.8 %iota_compare_fusion = pred[8,128]{1,0:T(8,128)(4,1)S(1)} fusion(s32[8]{0:T(128)} %param.19), kind=kLoop, calls=%fused_computation.23 | loop fusion | flops 1024 | bytes 1056 | tf_op jit(solution)/shard_map/lt | solution.py:34
  0.8 1.0 %fusion.9 = f32[8,4,1,8]{3,2,1,0:T(1,128)S(1)} fusion(bf16[8,4,8,128]{3,0,2,1:T(8,128)(2,1)} %bitcast.34, bf16[8,4,128,1]{2,0,1,3:T(8,128)(2,1)} %bitcast.39), kind=kOutput, calls=%fused_computation.14 | convolution fusion | flops 65536 | bytes 74752 | tf_op jit(solution)/shard_map/rkgd,rkd->rkg/dot_general | solution.py:31
  1.8 0.7 bitcast_convert_fusion
  2.5 0.0 copy-done
  2.5 1.6 %fusion.15 = (f32[8,4,8]{2,1,0:T(4,128)S(1)}, f32[8,4,8,128]{3,2,1,0:T(8,128)S(1)}) fusion(bf16[8,4,8,128]{3,0,2,1:T(8,128)(2,1)} %bitcast.35, pred[8,128]{1,0:T(8,128)(4,1)S(1)} %iota_compare_fusion, bf16[8,128,512]{2,1,0:T(8,128)(2,1)S(1)} %copy-done), kind=kOutput, calls=%fused_computation.25 | convolution fusion | flops 8486656 | bytes 1247232 | tf_op jit(solution)/shard_map/rkgd,rtkd->rkgt/dot_general | solution.py:27
  4.1 0.2 fusion.6
  4.4 1.7 %fusion.1 = bf16[8,4,8,128]{3,2,1,0:T(8,128)(2,1)S(1)} fusion(f32[8,4,8,128]{3,2,1,0:T(8,128)S(1)} %get-tuple-element.8, f32[8,4,128]{2,1,0:T(4,128)S(1)} %copy.18, f32[8,4,8]{2,1,0:T(4,128)S(1)} %get-tuple-element.6, f32[8,4,8]{2,1,0:T(4,128)S(1)} %get-tuple-element.5, f32[8,4,8]{2,1,0:T(4,128)S(1)} %multiply_maximum_fusion, bf16[8,128,512]{2,1,0:T(8,128)(2,1)} %param.16), kind=kOutput, calls=%fused_computation.3 | convolution fusion | flops 8585216 | bytes 1264640 | tf_op jit(solution)/shard_map/rkgt,rtkd->rkgd/dot_general | solution.py:42
  6.1 0.7 copy.43
  6.7 62.6 %shard_map.136 = bf16[8,4096]{1,0:T(8,128)(2,1)} custom-call(bf16[16,2048]{1,0:T(8,128)(2,1)} %bitcast.33, bf16[8,4096]{1,0:T(8,128)(2,1)} %residual_ref.1, s32[8,8]{1,0:T(8,128)} %ids_ref.1, f32[8,8]{1,0:T(8,128)} %mix_ref.1, bf16[4096,256]{1,0:T(8,128)(2,1)} %proj_ref.1, f32[1,4096]{1,0:T(1,128)} %bitcast.38, bf16[8,4096,384]{2,1,0:T(8,128)(2,1)} %wg_ref.1, ...), custom_call_target="tpu_custom_call" | custom-call | tf_op jit(solution)/shard_map/pallas_call | solution.py:479
  69.3 1.5 %copy.45 = bf16[8,4096]{1,0:T(8,128)(2,1)} copy(bf16[8,4096]{1,0:T(8,128)(2,1)} %shard_map.136) | data formatting | bytes 131072
  (4 shorter events, 0.1 us)
Async XLA Ops:
  0.0 2.5 %copy-start = (bf16[8,128,512]{2,1,0:T(8,128)(2,1)S(1)}, bf16[8,128,512]{2,1,0:T(8,128)(2,1)}, u32[]{:S(2)}) copy-start(bf16[8,128,512]{2,1,0:T(8,128)(2,1)} %param.15) | copy-start | bytes 3145732

commit v3 on v2

--- a/solution.py
+++ b/solution.py
@@ -149,6 +149,7 @@
     normed,
     activation,
     part,
+    early,
     got_core,
     got_row,
     got_col,
@@ -314,39 +315,66 @@
     lane = lax.broadcasted_iota(jnp.int32, (tokens, 128), 1)
 
     squares = [jnp.zeros((tokens, columns), jnp.float32)]
-
-    def add_squares(rank):
+    seen = []
+    ready = min(GATE_SLOTS, slots)
+    group = roles * columns
+
+    def use(rank):
         block = hid_all[rank].astype(jnp.float32)
         squares[0] = squares[0] + block * block
-
-    started += gather(hid_all, hid_send, hid_recv, add_squares)
+        cols = pl.ds(pl.multiple_of(rank * columns, columns), columns)
+        normed[:, cols] = (block * gain_ref[:, cols]).astype(jnp.bfloat16)
+        seen.append(rank)
+        if len(seen) % roles:
+            return
+        owner = (dev, across, sibling, diagonal)[len(seen) // roles - 1]
+        part_of = pl.ds(pl.multiple_of(owner * group, group), group)
+        opening = len(seen) == roles
+
+        def one_slot(slot, carry):
+            if opening:
+                for copy in gate_copies(slot, slot):
+                    copy.wait()
+            piece = jnp.dot(
+                normed[:, part_of],
+                gate_up[slot, part_of, :],
+                preferred_element_type=jnp.float32,
+            )
+            early[slot] = piece if opening else early[slot] + piece
+            return carry
+
+        lax.fori_loop(0, ready, one_slot, 0)
+
+    started += gather(hid_all, hid_send, hid_recv, use)
+    for s in range(ready, slots):
+        for copy in gate_copies(s, s - ready):
+            copy.start()
     mean = jnp.sum(squares[0], axis=1, keepdims=True) / width
     scale = lax.rsqrt(mean + 1e-06)
 
-    for k in range(devices):
-        cols = slice(k * columns, (k + 1) * columns)
-        block = hid_all[k].astype(jnp.float32)
-        normed[:, cols] = (block * scale * gain_ref[:, cols]).astype(jnp.bfloat16)
-
-    def one_half(s, carry):
+    def activate(s, both):
         expert = me * pairs + s // 2
         weight = jnp.sum(jnp.where(lane == expert, weights, 0.0), axis=1, keepdims=True)
-        slot = lax.rem(s, GATE_SLOTS)
+        gate = both[:, :half] * scale
+        value = gate / (1.0 + jnp.exp(-gate)) * (both[:, half:] * scale) * weight
+        activation[:, pl.ds(pl.multiple_of(s * half, 128), half)] = value.astype(jnp.bfloat16)
+
+    def from_early(s, carry):
+        activate(s, early[s])
+        return carry
+
+    lax.fori_loop(0, ready, from_early, 0)
+
+    def from_late(s, carry):
+        slot = s - ready
         for copy in gate_copies(s, slot):
             copy.wait()
-        both = jnp.dot(normed[...], gate_up[slot], preferred_element_type=jnp.float32)
-        gate = both[:, :half]
-        value = gate / (1.0 + jnp.exp(-gate)) * both[:, half:] * weight
-        activation[:, pl.ds(pl.multiple_of(s * half, 128), half)] = value.astype(jnp.bfloat16)
-
-        @pl.when(s + GATE_SLOTS < slots)
-        def _():
-            for copy in gate_copies(s + GATE_SLOTS, slot):
-                copy.start()
-
+        activate(
+            s, jnp.dot(normed[...], gate_up[slot], preferred_element_type=jnp.float32)
+        )
         return carry
 
-    lax.fori_loop(0, slots, one_half, 0)
+    lax.fori_loop(ready, slots, from_late, 0)
 
     to_core, to_row, to_col = {}, {}, {}
 
@@ -490,6 +518,7 @@
             pltpu.VMEM((tokens, width), bf16),
             pltpu.VMEM((tokens, slots * half), bf16),
             pltpu.VMEM((CHUNKS, 4, roles, 16, span), bf16),
+            pltpu.VMEM((min(GATE_SLOTS, slots), tokens, 2 * half), jnp.float32),
             pltpu.VMEM((CHUNKS, 2, roles, 16, span), bf16),
             pltpu.VMEM((CHUNKS, roles, 16, span), bf16),
             pltpu.VMEM((CHUNKS, roles - 1, 16, span), bf16),

time: 71.1 us -> 74.2 us (1.044)
  Pallas kernels: 62.6 us -> 65.6 us
    pallas_call x1, Pallas kernels: 62.6 us -> 65.6 us  [fused_body(): pl.pallas_call(functools.partial(layer_kernel, roles), out_shape=jax.Shap...]
where the time goes in v3:
time: 74.2 us; the launch traced here: 73.8 us
  Pallas kernels  65.6 us (88%)
  matrix products  4.23 us (6%)
  local copies, waits for them, and re-layouts  2.17 us (3%)
  other arithmetic  1.78 us (2%)
    pallas_call x1, Pallas kernels, fused_body(): pl.pallas_call(functools.partial(layer_kernel, roles), out_shape=jax.Shap...  65.6 us
    dot_general x1, matrix products, attend_rows(): jnp.einsum('rkgt,rtkd->rkgd', probs, cached_values, preferred_element_typ...  1.67 us
    dot_general x1, matrix products, attend_rows(): jnp.einsum('rkgd,rtkd->rkgt', grouped, cached_keys, preferred_element_typ...  1.56 us

profile of v3, /device:TPU:0, one launch (start us, length us, event | category | flops | bytes accessed | tf_op | source)
XLA Modules:
  0.0 73.8 jit_solution(7877076686902527376)
XLA Ops:
  0.0 0.0 copy-start
  0.0 0.8 %iota_compare_fusion = pred[8,128]{1,0:T(8,128)(4,1)S(1)} fusion(s32[8]{0:T(128)} %param.19), kind=kLoop, calls=%fused_computation.23 | loop fusion | flops 1024 | bytes 1056 | tf_op jit(solution)/shard_map/lt | solution.py:34
  0.8 1.0 %fusion.9 = f32[8,4,1,8]{3,2,1,0:T(1,128)S(1)} fusion(bf16[8,4,8,128]{3,0,2,1:T(8,128)(2,1)} %bitcast.34, bf16[8,4,128,1]{2,0,1,3:T(8,128)(2,1)} %bitcast.39), kind=kOutput, calls=%fused_computation.14 | convolution fusion | flops 65536 | bytes 74752 | tf_op jit(solution)/shard_map/rkgd,rkd->rkg/dot_general | solution.py:31
  1.8 0.7 bitcast_convert_fusion
  2.5 0.0 copy-done
  2.5 1.6 %fusion.15 = (f32[8,4,8]{2,1,0:T(4,128)S(1)}, f32[8,4,8,128]{3,2,1,0:T(8,128)S(1)}) fusion(bf16[8,4,8,128]{3,0,2,1:T(8,128)(2,1)} %bitcast.35, pred[8,128]{1,0:T(8,128)(4,1)S(1)} %iota_compare_fusion, bf16[8,128,512]{2,1,0:T(8,128)(2,1)S(1)} %copy-done), kind=kOutput, calls=%fused_computation.25 | convolution fusion | flops 8486656 | bytes 1247232 | tf_op jit(solution)/shard_map/rkgd,rtkd->rkgt/dot_general | solution.py:27
  4.1 0.2 fusion.6
  4.4 1.7 %fusion.1 = bf16[8,4,8,128]{3,2,1,0:T(8,128)(2,1)S(1)} fusion(f32[8,4,8,128]{3,2,1,0:T(8,128)S(1)} %get-tuple-element.8, f32[8,4,128]{2,1,0:T(4,128)S(1)} %copy.18, f32[8,4,8]{2,1,0:T(4,128)S(1)} %get-tuple-element.6, f32[8,4,8]{2,1,0:T(4,128)S(1)} %get-tuple-element.5, f32[8,4,8]{2,1,0:T(4,128)S(1)} %multiply_maximum_fusion, bf16[8,128,512]{2,1,0:T(8,128)(2,1)} %param.16), kind=kOutput, calls=%fused_computation.3 | convolution fusion | flops 8585216 | bytes 1264640 | tf_op jit(solution)/shard_map/rkgt,rtkd->rkgd/dot_general | solution.py:42
  6.1 0.7 copy.43
  6.7 65.6 %shard_map.136 = bf16[8,4096]{1,0:T(8,128)(2,1)} custom-call(bf16[16,2048]{1,0:T(8,128)(2,1)} %bitcast.33, bf16[8,4096]{1,0:T(8,128)(2,1)} %residual_ref.1, s32[8,8]{1,0:T(8,128)} %ids_ref.1, f32[8,8]{1,0:T(8,128)} %mix_ref.1, bf16[4096,256]{1,0:T(8,128)(2,1)} %proj_ref.1, f32[1,4096]{1,0:T(1,128)} %bitcast.38, bf16[8,4096,384]{2,1,0:T(8,128)(2,1)} %wg_ref.1, ...), custom_call_target="tpu_custom_call" | custom-call | tf_op jit(solution)/shard_map/pallas_call | solution.py:507
  72.4 1.5 %copy.45 = bf16[8,4096]{1,0:T(8,128)(2,1)} copy(bf16[8,4096]{1,0:T(8,128)(2,1)} %shard_map.136) | data formatting | bytes 131072
  (4 shorter events, 0.1 us)
Async XLA Ops:
  0.0 2.5 %copy-start = (bf16[8,128,512]{2,1,0:T(8,128)(2,1)S(1)}, bf16[8,128,512]{2,1,0:T(8,128)(2,1)}, u32[]{:S(2)}) copy-start(bf16[8,128,512]{2,1,0:T(8,128)(2,1)} %param.15) | copy-start | bytes 3145732
